TPU v7x, 32 devices: a whole 2x2x4 slice. The times are simulated.
32 devices in a mesh: rows: 4 (over y, core), cent: 8 (over z, x).
Axes of the slice: x: 2, y: 2, z: 4, core: 2. Of those that a mesh axis runs over, the one named last changes fastest.
Arguments:
- embeddings: bfloat16 [256, 1024], P(('rows', 'cent')), may hold values from -36 to 36
- centroids: bfloat16 [32768, 1024], P(('rows', 'cent')), may hold values from -1 to 1
Outputs:
- row_lse: float32 [256], P(('rows', 'cent'))
- weighted_sums: bfloat16 [32768, 1024], P(('rows', 'cent'))
- counts: float32 [32768], P(('rows', 'cent'))
All inputs are finite; a program needn't handle non-finite values.
Results may differ from a plain program's by a relative error of at most 0.0075.
Values may be sent and summed in bfloat16 or wider, within the bound.
A program may use at most 64 MiB of HBM per device.

v0:
```python
import jax
import jax.numpy as jnp
from jax import lax
from jax.sharding import PartitionSpec as P

inverse_temp = 3.0


def score_block(piece, centroids):
    return inverse_temp * lax.dot_general(
        piece, centroids, (((1,), (1,)), ((), ())), preferred_element_type=jnp.float32
    )


def on_device(embeddings, centroids):
    local_rows = embeddings.shape[0]
    gathered = lax.all_gather(embeddings, ("rows", "cent"), axis=0, tiled=True)
    scores = score_block(gathered, centroids)
    local_max = jnp.max(scores, axis=1)
    largest = lax.pmax(local_max, ("rows", "cent"))
    local_total = jnp.sum(jnp.exp(scores - largest[:, None]), axis=1)
    total = lax.psum(local_total, ("rows", "cent"))
    row_lse = largest + jnp.log(total)
    resp = jnp.exp(scores - row_lse[:, None]).astype(jnp.bfloat16)
    counts = jnp.sum(resp, axis=0, dtype=jnp.float32)
    sums = lax.dot_general(
        resp, gathered, (((0,), (0,)), ((), ())), preferred_element_type=jnp.float32
    )
    offset = lax.axis_index(("rows", "cent")) * local_rows
    own_lse = lax.dynamic_slice_in_dim(row_lse, offset, local_rows, 0)
    return (own_lse, sums.astype(jnp.bfloat16), counts)


def solution(mesh):
    return jax.shard_map(
        on_device,
        mesh=mesh,
        in_specs=(P(("rows", "cent"), None), P(("rows", "cent"), None)),
        out_specs=(P(("rows", "cent")), P(("rows", "cent"), None), P(("rows", "cent"))),
        check_vma=False,
    )
```

profile of v0, /device:TPU:0, one launch (start us, length us, event | category | flops | bytes accessed | tf_op | source)
XLA Modules:
  0.0 158.6 jit_solution(17720211279837233537)
XLA Ops:
  0.6 0.0 copy-start
  0.6 73.4 %all_gather.3 = bf16[256,1024]{1,0:T(8,128)(2,1)S(1)} all-gather(bf16[8,1024]{1,0:T(8,128)(2,1)} %param.2), channel_id=1, replica_groups=mesh['rows'=4,'cent'=8] {'rows','cent'}, dimensions={0}, use_global_device_ids=true | all-gather | bytes 540672 | tf_op jit(solution)/shard_map/all_gather | solution.py:17
  74.0 0.0 copy-start.1
  74.0 0.8 copy-done.1
  74.8 0.0 copy-done
  74.8 0.8 fusion
  75.6 36.9 %pmax.7 = f32[256]{0:T(256)S(1)} all-reduce(f32[256]{0:T(256)S(1)} %get-tuple-element.3), channel_id=1, replica_groups=mesh['rows'=4,'cent'=8] {'rows','cent'}, use_global_device_ids=true, to_apply=%region_1.0 | all-reduce | flops 256 | bytes 2048 | tf_op jit(solution)/shard_map/pmax | solution.py:20
  112.5 0.3 exponential_reduce_fusion
  112.8 41.1 %psum.7 = f32[256]{0:T(256)S(1)} all-reduce(f32[256]{0:T(256)S(1)} %exponential_reduce_fusion), channel_id=1, replica_groups=mesh['rows'=4,'cent'=8] {'rows','cent'}, use_global_device_ids=true, to_apply=%region_3.0 | all-reduce | flops 256 | bytes 2048 | tf_op jit(solution)/shard_map/psum | solution.py:22
  154.0 0.6 dynamic_slice.3
  154.6 3.2 %convolution_convert_fusion = bf16[1024,1024]{1,0:T(8,128)(2,1)} fusion(bf16[256,1024]{1,0:T(8,128)(2,1)} %copy-done.1, f32[256,1024]{1,0:T(8,128)S(1)} %get-tuple-element.4, f32[256]{0:T(256)S(1)} %log_add_fusion), kind=kOutput, calls=%fused_computation | convolution fusion | flops 538443776 | bytes 3671040 | tf_op jit(solution)/shard_map/dot_general | solution.py:26
  157.8 0.8 convert_reduce_fusion
  (1 shorter events, 0.0 us)
Async XLA Ops:
  0.6 74.2 %copy-start = (bf16[1024,1024]{1,0:T(8,128)(2,1)S(1)}, bf16[1024,1024]{1,0:T(8,128)(2,1)}, u32[]{:S(2)}) copy-start(bf16[1024,1024]{1,0:T(8,128)(2,1)} %param.3) | copy-start | bytes 6291460
  74.0 0.8 copy-start.1
where the time goes:
time: 159 us
  blocking collectives  151 us (95%)
  matrix products  4.02 us (3%)
    all_gather x1, blocking collectives, on_device(): gathered = lax.all_gather(embeddings, ('rows', 'cent'), axis=0, tiled=True)  73.4 us
    psum x1, blocking collectives, on_device(): total = lax.psum(local_total, ('rows', 'cent'))  41.1 us
    pmax x1, blocking collectives, on_device(): largest = lax.pmax(local_max, ('rows', 'cent'))  36.9 us
    dot_general x1, matrix products, on_device(): lax.dot_general(resp, gathered, (((0,), (0,)), ((), ())), preferred_eleme...  3.2 us

commit v1 on v0

v1 whole, which is shorter than its diff:
```python
import functools

import jax
import jax.numpy as jnp
from jax import lax
from jax.experimental import pallas as pl
from jax.experimental.pallas import tpu as pltpu
from jax.sharding import PartitionSpec as P

inverse_temp = 3.0
MESH = pl.DeviceIdType.MESH
NT = (((1,), (1,)), ((), ()))
NN = (((1,), (0,)), ((), ()))


def kernel(
    sizes, emb, cen, lse_out, counts_out, sums_out,
    cen_v, slots, gathered, shifted, resp, sums_v, stats,
    cen_sem, z_send, z_recv, p_send, p_recv, c_send, c_recv, s_send, s_recv, out_sem,
):
    Y, X, Z = sizes
    devices = 2 * Y * X * Z
    cents = X * Z
    n, depth = gathered.shape
    half = depth // 2
    k = cen.shape[0]
    r = lax.axis_index("rows")
    c = lax.axis_index("cent")
    y, core = r // 2, r % 2
    z, x = c // X, c % X

    def place(y_, core_, z_, x_):
        return (y_ * 2 + core_, z_ * X + x_)

    load = pltpu.make_async_copy(cen, cen_v, cen_sem)
    load.start()

    z_peers = [place(y, core, (z + i) % Z, x) for i in range(1, Z)]
    plane = [(i, j) for i in range(Y) for j in range(X) if (i, j) != (0, 0)]
    p_peers = [place((y + i) % Y, core, z, (x + j) % X) for i, j in plane]
    twin = place(y, 1 - core, z, x)

    barrier = pltpu.get_barrier_semaphore()
    for peer in z_peers + p_peers + [twin]:
        pl.semaphore_signal(barrier, inc=1, device_id=peer, device_id_type=MESH)

    def column(core_, y_, x_):
        return ((core_ * Y + y_) * X + x_) * Z

    base = column(core, y, x)
    mine = base + z
    own = emb[...].astype(jnp.float32)
    own = jnp.concatenate([own[:, :half], own[:, half:]], axis=0)
    slots[mine] = own.astype(jnp.bfloat16)
    pl.semaphore_wait(barrier, len(z_peers) + len(p_peers) + 1)

    def send(first, count, send_sem, recv_sem, peer):
        ref = slots.at[pl.ds(first, count)]
        return pltpu.make_async_remote_copy(
            src_ref=ref, dst_ref=ref, send_sem=send_sem, recv_sem=recv_sem,
            device_id=peer, device_id_type=MESH,
        )

    z_copies = [
        send(mine, 1, z_send.at[i], z_recv.at[i], peer) for i, peer in enumerate(z_peers)
    ]
    for copy in z_copies:
        copy.start()
    for copy in z_copies:
        copy.wait_recv()
    p_copies = [
        send(base, Z, p_send.at[i], p_recv.at[i], peer) for i, peer in enumerate(p_peers)
    ]
    for copy in p_copies:
        copy.start()
    c_copies = [send(base, Z, c_send.at[0], c_recv.at[0], twin)]
    c_copies[0].start()
    for i, (copy, (dy, dx)) in enumerate(zip(p_copies, plane)):
        copy.wait_recv()
        first = column(core, (y - dy + Y) % Y, (x - dx + X) % X)
        c_copies.append(send(first, Z, c_send.at[i + 1], c_recv.at[i + 1], twin))
        c_copies[-1].start()
    for copy in c_copies:
        copy.wait_recv()
    for copy in z_copies + p_copies + c_copies:
        copy.wait_send()

    step = min(8, devices)

    @pl.loop(0, devices // step)
    def _(i):
        part = slots[pl.ds(i * step, step)].astype(jnp.float32)
        rows = pl.ds(pl.multiple_of(i * step * 8, step * 8), step * 8)
        gathered[rows, :half] = part[:, :8].reshape(step * 8, half).astype(jnp.bfloat16)
        gathered[rows, half:] = part[:, 8:].reshape(step * 8, half).astype(jnp.bfloat16)

    load.wait()

    tile = 256
    wide = min(n, 256)

    @pl.loop(0, n // wide)
    def _(j):
        lanes = pl.ds(pl.multiple_of(j * wide, wide), wide)
        top = jnp.full((8, wide), -jnp.inf, jnp.float32)
        for t in range(k // tile):
            rows = pl.ds(t * tile, tile)
            part = inverse_temp * lax.dot_general(
                cen_v[rows, :], gathered[lanes, :], NT, preferred_element_type=jnp.float32
            )
            shifted[rows, lanes] = part
            top = jnp.maximum(top, jnp.max(part.reshape(tile // 8, 8, wide), axis=0))
        top = jnp.max(top, axis=0, keepdims=True)
        total = jnp.zeros((8, wide), jnp.float32)
        for t in range(k // tile):
            rows = pl.ds(t * tile, tile)
            part = jnp.exp(shifted[rows, lanes] - top)
            shifted[rows, lanes] = part
            total = total + jnp.sum(part.reshape(tile // 8, 8, wide), axis=0)
        stats[r * cents + c, 0:1, lanes] = top
        stats[r * cents + c, 1:2, lanes] = jnp.sum(total, axis=0, keepdims=True)

    me = r * cents + c

    def stat_copy(i):
        peer = (me + i) % devices
        return pltpu.make_async_remote_copy(
            src_ref=stats.at[me], dst_ref=stats.at[me], send_sem=s_send, recv_sem=s_recv,
            device_id=(peer // cents, peer % cents), device_id_type=MESH,
        )

    @pl.loop(1, devices)
    def _(i):
        stat_copy(i).start()

    others = stats.at[pl.ds(0, devices - 1)]
    pltpu.make_async_copy(others, others, s_recv).wait()

    @pl.loop(0, n // wide)
    def _(j):
        lanes = pl.ds(pl.multiple_of(j * wide, wide), wide)
        tops = stats[:, 0:1, lanes]
        top = jnp.max(tops, axis=0)
        total = jnp.sum(stats[:, 1:2, lanes] * jnp.exp(tops - top[None]), axis=0)
        lse = top + jnp.log(total)
        lse_out[:, lanes] = lse
        factor = jnp.exp(stats[me, 0:1, lanes] - lse)
        for t in range(k // tile):
            rows = pl.ds(t * tile, tile)
            resp[rows, lanes] = (shifted[rows, lanes] * factor).astype(jnp.bfloat16)

    counts_out[...] = lax.dot_general(
        jnp.ones((8, n), jnp.bfloat16), resp[...], NT, preferred_element_type=jnp.float32
    )[0:1]

    outs = []
    for t in range(k // tile):
        rows = pl.ds(t * tile, tile)
        sums_v[rows, :] = lax.dot_general(
            resp[rows, :], gathered[...], NN, preferred_element_type=jnp.float32
        ).astype(jnp.bfloat16)
        outs.append(pltpu.make_async_copy(sums_v.at[rows], sums_out.at[rows], out_sem.at[t]))
        outs[-1].start()
    pltpu.make_async_copy(others, others, s_send).wait()
    for copy in outs:
        copy.wait()


def on_device(sizes, embeddings, centroids):
    Y, X, Z = sizes
    devices = 2 * Y * X * Z
    local, depth = embeddings.shape
    k = centroids.shape[0]
    n = local * devices
    dma = pltpu.SemaphoreType.DMA
    planes = Y * X - 1
    vmem = pl.BlockSpec(memory_space=pltpu.VMEM)
    lse, counts, sums = pl.pallas_call(
        functools.partial(kernel, sizes),
        out_shape=(
            jax.ShapeDtypeStruct((1, n), jnp.float32),
            jax.ShapeDtypeStruct((1, k), jnp.float32),
            jax.ShapeDtypeStruct((k, depth), jnp.bfloat16),
        ),
        in_specs=[vmem, pl.BlockSpec(memory_space=pl.ANY)],
        out_specs=(vmem, vmem, pl.BlockSpec(memory_space=pl.ANY)),
        scratch_shapes=[
            pltpu.VMEM((k, depth), jnp.bfloat16),
            pltpu.VMEM((devices, 2 * local, depth // 2), jnp.bfloat16),
            pltpu.VMEM((n, depth), jnp.bfloat16),
            pltpu.VMEM((k, n), jnp.float32),
            pltpu.VMEM((k, n), jnp.bfloat16),
            pltpu.VMEM((k, depth), jnp.bfloat16),
            pltpu.VMEM((devices, 2, n), jnp.float32),
            dma,
            dma((Z - 1,)), dma((Z - 1,)),
            dma((planes,)), dma((planes,)),
            dma((planes + 1,)), dma((planes + 1,)),
            dma, dma,
            dma((k // 256,)),
        ],
        compiler_params=pltpu.CompilerParams(
            collective_id=0, has_side_effects=True, vmem_limit_bytes=48 * 2**20
        ),
    )(embeddings, centroids)
    y, core = lax.axis_index("rows") // 2, lax.axis_index("rows") % 2
    z, x = lax.axis_index("cent") // X, lax.axis_index("cent") % X
    slot = ((core * Y + y) * X + x) * Z + z
    own_lse = lax.dynamic_slice_in_dim(lse.reshape(n), slot * local, local, 0)
    return own_lse, sums, counts.reshape(k)


def solution(mesh):
    rows, cents = mesh.shape["rows"], mesh.shape["cent"]
    Y = rows // 2
    X = Y if cents % Y == 0 else 1
    return jax.shard_map(
        functools.partial(on_device, (Y, X, cents // X)),
        mesh=mesh,
        in_specs=(P(("rows", "cent"), None), P(("rows", "cent"), None)),
        out_specs=(P(("rows", "cent")), P(("rows", "cent"), None), P(("rows", "cent"))),
        check_vma=False,
    )
```

time: 159 us -> 28.2 us (0.18)
  blocking collectives: 151 us -> 0 us
  Pallas kernels: 0 us -> 22.5 us
  matrix products: 4.02 us -> 0 us
  local copies, waits for them, and re-layouts: 1.39 us -> 4.8 us
    all_gather x1 -> x0, blocking collectives: 73.4 us -> none  [on_device(): gathered = lax.all_gather(embeddings, ('rows', 'cent'), axis=0, tiled=True)]
    psum x1 -> x0, blocking collectives: 41.1 us -> none  [on_device(): total = lax.psum(local_total, ('rows', 'cent'))]
    pmax x1 -> x0, blocking collectives: 36.9 us -> none  [on_device(): largest = lax.pmax(local_max, ('rows', 'cent'))]
    pallas_call x0 -> x1, Pallas kernels: none -> 22.5 us  [on_device(): pl.pallas_call(functools.partial(kernel, sizes), out_shape=(jax.ShapeDtyp...]
    dot_general x2 -> x0, matrix products: 4.02 us -> none  [the longest x1 3.2 us: on_device(): lax.dot_general(resp, gathered, (((0,), (0,)), ((), ())), preferred_eleme...]
    unnamed x4 -> x6, local copies, waits for them, and re-layouts: 0.8 us -> 4.21 us
where the time goes in v1:
time: 28.2 us; the launch traced here: 28 us
  Pallas kernels  22.5 us (80%)
  local copies, waits for them, and re-layouts  4.8 us (17%)
  between operations  0.69 us (2%)
    pallas_call x1, Pallas kernels, on_device(): pl.pallas_call(functools.partial(kernel, sizes), out_shape=(jax.ShapeDtyp...  22.5 us
    unnamed x6, local copies, waits for them, and re-layouts  4.21 us
    dynamic_slice x1, local copies, waits for them, and re-layouts, on_device(): own_lse = lax.dynamic_slice_in_dim(lse.reshape(n), slot * local, local, 0)  0.59 us

profile of v1, /device:TPU:0, one launch (start us, length us, event | category | flops | bytes accessed | tf_op | source)
XLA Modules:
  0.0 28.0 jit_solution(2979802782559019983)
XLA Ops:
  0.7 0.0 copy-start
  0.7 1.6 %copy-done = bf16[1024,1024]{1,0:T(8,128)(2,1)S(1)} copy-done((bf16[1024,1024]{1,0:T(8,128)(2,1)S(1)}, bf16[1024,1024]{1,0:T(8,128)(2,1)}, u32[]{:S(2)}) %copy-start) | copy-done | bytes 2097176
  2.3 0.0 copy-start.1
  2.3 0.7 %copy-done.1 = bf16[8,1024]{1,0:T(8,128)(2,1)S(1)} copy-done((bf16[8,1024]{1,0:T(8,128)(2,1)S(1)}, bf16[8,1024]{1,0:T(8,128)(2,1)}, u32[]{:S(2)}) %copy-start.1) | copy-done | bytes 16408
  3.0 22.5 %shard_map.49 = (f32[1,256]{1,0:T(1,128)S(1)}, f32[1,1024]{1,0:T(1,128)S(1)}, bf16[1024,1024]{1,0:T(8,128)(2,1)S(1)}) custom-call(bf16[8,1024]{1,0:T(8,128)(2,1)S(1)} %copy-done.1, bf16[1024,1024]{1,0:T(8,128)(2,1)S(1)} %copy-done), custom_call_target="tpu_custom_call" | custom-call | tf_op jit(solution)/shard_map/pallas_call | solution.py:178
  25.5 0.6 %dynamic-slice_bitcast_fusion = f32[8]{0:T(128)} fusion(f32[1,256]{1,0:T(1,128)S(1)} %get-tuple-element.6, s32[]{:T(128)S(6)} %select_n.25), kind=kLoop, calls=%fused_computation | loop fusion | bytes 68 | tf_op jit(solution)/shard_map/dynamic_slice | solution.py:209
  26.1 1.3 %copy.7 = bf16[1024,1024]{1,0:T(8,128)(2,1)} copy(bf16[1024,1024]{1,0:T(8,128)(2,1)S(1)} %get-tuple-element.13) | data formatting | bytes 4194304
  27.4 0.6 %copy.8 = f32[1024]{0:T(1024)} copy(f32[1024]{0:T(1024)S(1)} %bitcast.3) | data formatting | bytes 8192
Async XLA Ops:
  0.7 1.6 %copy-start = (bf16[1024,1024]{1,0:T(8,128)(2,1)S(1)}, bf16[1024,1024]{1,0:T(8,128)(2,1)}, u32[]{:S(2)}) copy-start(bf16[1024,1024]{1,0:T(8,128)(2,1)} %cen.1) | copy-start | bytes 6291460
  2.3 0.7 %copy-start.1 = (bf16[8,1024]{1,0:T(8,128)(2,1)S(1)}, bf16[8,1024]{1,0:T(8,128)(2,1)}, u32[]{:S(2)}) copy-start(bf16[8,1024]{1,0:T(8,128)(2,1)} %emb.1) | copy-start | bytes 49156

commit v2 on v1

v2 whole, which is shorter than its diff:
```python
import functools

import jax
import jax.numpy as jnp
from jax import lax
from jax.experimental import pallas as pl
from jax.experimental.pallas import tpu as pltpu
from jax.sharding import PartitionSpec as P

inverse_temp = 3.0
MESH = pl.DeviceIdType.MESH
NT = (((1,), (1,)), ((), ()))
SUMS_TILE = 256
NN = (((1,), (0,)), ((), ()))


def flipped(index, size, mask):
    if size & (size - 1):
        return (index + mask) % size
    bit = 1
    while bit < size:
        if mask & bit:
            index = index + bit - 2 * bit * ((index // bit) % 2)
        bit *= 2
    return index


def sender(index, size, mask):
    if size & (size - 1):
        return (index + size - mask) % size
    return flipped(index, size, mask)


def spread_kernel(
    sizes, emb, cen, lse_out, resp, gathered,
    cen_v, slots, shifted, stats,
    own_sem, cen_sem, b_send, b_recv, c_send, c_recv, s_send, s_recv,
):
    Y, X, Z = sizes
    devices = 2 * Y * X * Z
    cents = X * Z
    n = gathered.shape[0]
    local = emb.shape[0]
    k = cen.shape[0]
    r = lax.axis_index("rows")
    c = lax.axis_index("cent")
    y, core = r // 2, r % 2
    z, x = c // X, c % X

    def place(y_, core_, z_, x_):
        return (y_ * 2 + core_, z_ * X + x_)

    def slot_of(y_, core_, z_, x_):
        return ((core_ * Y + y_) * X + x_) * Z + z_

    plane = [(i, j) for i in range(Y) for j in range(X)]
    z_peers = [place(y, core, flipped(z, Z, i), x) for i in range(Z)]
    p_peers = [place(flipped(y, Y, i), core, z, flipped(x, X, j)) for i, j in plane]
    twin = place(y, 1 - core, z, x)

    barrier = pltpu.get_barrier_semaphore()
    for peer in z_peers[1:] + p_peers[1:] + [twin]:
        pl.semaphore_signal(barrier, inc=1, device_id=peer, device_id_type=MESH)
    mine = slot_of(y, core, z, x)
    load_own = pltpu.make_async_copy(emb, slots.at[mine], own_sem)
    load_own.start()
    load = pltpu.make_async_copy(cen, cen_v, cen_sem)
    load.start()
    pl.semaphore_wait(barrier, len(z_peers) + len(p_peers) - 1)

    def send(src, slot, sems, peer):
        return pltpu.make_async_remote_copy(
            src_ref=src, dst_ref=slots.at[slot], send_sem=sems[0], recv_sem=sems[1],
            device_id=peer, device_id_type=MESH,
        )

    def link_sems(i, p):
        return b_send.at[i, p], b_recv.at[i, p]

    def block_slot(i, p):
        dy, dx = plane[p]
        return slot_of(sender(y, Y, dy), core, sender(z, Z, i), sender(x, X, dx))

    started = []
    def start(copy):
        copy.start()
        started.append(copy)
        return copy

    def to_plane(i, src):
        return [
            start(send(src, block_slot(i, 0), link_sems(i, p), p_peers[p]))
            for p in range(1, len(plane))
        ]

    def to_twin(i, p, src):
        return start(send(src, block_slot(i, p), (c_send.at[i, p], c_recv.at[i, p]), twin))

    arrivals = {}
    for i in range(Z - 1, 0, -1):
        arrivals[i, 0] = start(send(emb, mine, link_sems(i, 0), z_peers[i]))
    for p, copy in enumerate(to_plane(0, emb)):
        arrivals[0, p + 1] = copy
    over = [to_twin(0, 0, emb)]
    for i in range(1, Z):
        arrivals[i, 0].wait_recv()
        src = slots.at[block_slot(i, 0)]
        for p, copy in enumerate(to_plane(i, src)):
            arrivals[i, p + 1] = copy
        over.append(to_twin(i, 0, src))
    for i in range(Z):
        for p in range(1, len(plane)):
            arrivals[i, p].wait_recv()
            over.append(to_twin(i, p, slots.at[block_slot(i, p)]))
    load_own.wait()

    step = min(8, devices // 2)

    def lay_out(first):
        @pl.loop(0, devices // 2 // step)
        def _(i):
            part = slots[pl.ds(first + i * step, step)].astype(jnp.float32)
            rows = pl.ds(pl.multiple_of((first + i * step) * local, step * local), step * local)
            gathered[rows, :] = part.reshape(step * local, part.shape[2]).astype(jnp.bfloat16)

    lay_out(core * (devices // 2))
    load.wait()
    for copy in over:
        copy.wait_recv()
    lay_out((1 - core) * (devices // 2))
    tile = 256
    wide = min(n, 256)
    me = r * cents + c

    @pl.loop(0, n // wide)
    def _(j):
        lanes = pl.ds(pl.multiple_of(j * wide, wide), wide)
        top = jnp.full((8, wide), -jnp.inf, jnp.float32)
        for t in range(k // tile):
            rows = pl.ds(t * tile, tile)
            part = inverse_temp * lax.dot_general(
                cen_v[rows, :], gathered[lanes, :], NT, preferred_element_type=jnp.float32
            )
            shifted[rows, lanes] = part
            top = jnp.maximum(top, jnp.max(part.reshape(tile // 8, 8, wide), axis=0))
        top = jnp.max(top, axis=0, keepdims=True)
        total = jnp.zeros((8, wide), jnp.float32)
        for t in range(k // tile):
            rows = pl.ds(t * tile, tile)
            part = jnp.exp(shifted[rows, lanes] - top)
            shifted[rows, lanes] = part
            total = total + jnp.sum(part.reshape(tile // 8, 8, wide), axis=0)
        stats[me, 0:1, lanes] = top
        stats[me, 1:2, lanes] = jnp.sum(total, axis=0, keepdims=True)

    offsets = [
        (i, j, l, m) for l in range(Z) for i in range(Y) for j in range(X) for m in range(2)
    ]
    for i, j, l, m in reversed(offsets[1:]):
        peer = place(flipped(y, Y, i), (core + m) % 2, flipped(z, Z, l), flipped(x, X, j))
        pltpu.make_async_remote_copy(
            src_ref=stats.at[me], dst_ref=stats.at[me], send_sem=s_send, recv_sem=s_recv,
            device_id=peer, device_id_type=MESH,
        ).start()
    for copy in started:
        copy.wait_send()

    others = stats.at[pl.ds(0, devices - 1)]
    pltpu.make_async_copy(others, others, s_recv).wait()

    @pl.loop(0, n // wide)
    def _(j):
        lanes = pl.ds(pl.multiple_of(j * wide, wide), wide)
        tops = stats[:, 0:1, lanes]
        top = jnp.max(tops, axis=0)
        total = jnp.sum(stats[:, 1:2, lanes] * jnp.exp(tops - top[None]), axis=0)
        lse = top + jnp.log(total)
        lse_out[:, lanes] = lse
        factor = jnp.exp(stats[me, 0:1, lanes] - lse)
        for t in range(k // tile):
            rows = pl.ds(t * tile, tile)
            resp[rows, lanes] = (shifted[rows, lanes] * factor).astype(jnp.bfloat16)

    pltpu.make_async_copy(others, others, s_send).wait()


def sums_kernel(
    sizes, lse, resp, gathered, lse_out, counts_out, sums_out,
    lse_v, counts_v, sums_v, lse_sem, counts_sem, out_sem,
):
    Y, X, Z = sizes
    n = gathered.shape[0]
    k = resp.shape[0]
    local = lse_out.shape[1]
    r = lax.axis_index("rows")
    c = lax.axis_index("cent")
    slot = (((r % 2) * Y + r // 2) * X + c % X) * Z + c // X

    outs = []
    for t in range(k // SUMS_TILE):
        rows = pl.ds(t * SUMS_TILE, SUMS_TILE)
        sums_v[rows, :] = lax.dot_general(
            resp[rows, :], gathered[...], NN, preferred_element_type=jnp.float32
        ).astype(jnp.bfloat16)
        outs.append(pltpu.make_async_copy(sums_v.at[rows], sums_out.at[rows], out_sem.at[t]))
        outs[-1].start()
        if t == 0:
            rolled = pltpu.roll(jnp.broadcast_to(lse[...], (8, n)), n - slot * local, 1)
            lse_v[...] = rolled[0:1, :local]
            outs.append(pltpu.make_async_copy(lse_v, lse_out, lse_sem))
            outs[-1].start()
            counts_v[...] = lax.dot_general(
                jnp.ones((8, n), jnp.bfloat16), resp[...], NT,
                preferred_element_type=jnp.float32,
            )[0:1]
            outs.append(pltpu.make_async_copy(counts_v, counts_out, counts_sem))
            outs[-1].start()
    for copy in outs:
        copy.wait()


def on_device(sizes, embeddings, centroids):
    Y, X, Z = sizes
    devices = 2 * Y * X * Z
    local, depth = embeddings.shape
    k = centroids.shape[0]
    n = local * devices
    dma = pltpu.SemaphoreType.DMA
    vmem = pl.BlockSpec(memory_space=pltpu.VMEM)
    hbm = pl.BlockSpec(memory_space=pltpu.HBM)
    embeddings = pltpu.with_memory_space_constraint(embeddings, pltpu.HBM)
    centroids = pltpu.with_memory_space_constraint(centroids, pltpu.HBM)
    lse, resp, gathered = pl.pallas_call(
        functools.partial(spread_kernel, sizes),
        out_shape=(
            jax.ShapeDtypeStruct((1, n), jnp.float32),
            jax.ShapeDtypeStruct((k, n), jnp.bfloat16),
            jax.ShapeDtypeStruct((n, depth), jnp.bfloat16),
        ),
        in_specs=[hbm, hbm],
        out_specs=(vmem, vmem, vmem),
        scratch_shapes=[
            pltpu.VMEM((k, depth), jnp.bfloat16),
            pltpu.VMEM((devices, local, depth), jnp.bfloat16),
            pltpu.VMEM((k, n), jnp.float32),
            pltpu.VMEM((devices, 2, n), jnp.float32),
            dma, dma,
            dma((Z, Y * X)), dma((Z, Y * X)),
            dma((Z, Y * X)), dma((Z, Y * X)),
            dma, dma,
        ],
        compiler_params=pltpu.CompilerParams(
            collective_id=0, has_side_effects=True, vmem_limit_bytes=32 * 2**20
        ),
    )(embeddings, centroids)
    own_lse, counts, sums = pl.pallas_call(
        functools.partial(sums_kernel, sizes),
        out_shape=(
            jax.ShapeDtypeStruct((1, local), jnp.float32),
            jax.ShapeDtypeStruct((1, k), jnp.float32),
            jax.ShapeDtypeStruct((k, depth), jnp.bfloat16),
        ),
        in_specs=[vmem, vmem, vmem],
        out_specs=(hbm, hbm, hbm),
        scratch_shapes=[
            pltpu.VMEM((1, local), jnp.float32),
            pltpu.VMEM((1, k), jnp.float32),
            pltpu.VMEM((k, depth), jnp.bfloat16),
            dma, dma,
            dma((k // SUMS_TILE,)),
        ],
        compiler_params=pltpu.CompilerParams(vmem_limit_bytes=16 * 2**20),
    )(lse, resp, gathered)
    return own_lse.reshape(local), sums, counts.reshape(k)


def solution(mesh):
    rows, cents = mesh.shape["rows"], mesh.shape["cent"]
    Y = rows // 2
    X = Y if cents % Y == 0 else 1
    return jax.shard_map(
        functools.partial(on_device, (Y, X, cents // X)),
        mesh=mesh,
        in_specs=(P(("rows", "cent"), None), P(("rows", "cent"), None)),
        out_specs=(P(("rows", "cent")), P(("rows", "cent"), None), P(("rows", "cent"))),
        check_vma=False,
    )
```

time: 28.2 us -> 22.3 us (0.79)
  local copies, waits for them, and re-layouts: 4.8 us -> 0 us
  Pallas kernels: 22.5 us -> 21.5 us
    unnamed x6 -> x0, local copies, waits for them, and re-layouts: 4.21 us -> none
    pallas_call x1 -> x2, Pallas kernels: 22.5 us -> 21.5 us  [the longest x1 19.7 us: on_device(): pl.pallas_call(functools.partial(spread_kernel, sizes), out_shape=(jax.Sh...]
    dynamic_slice x1 -> x0, local copies, waits for them, and re-layouts: 0.59 us -> none  [on_device(): own_lse = lax.dynamic_slice_in_dim(lse.reshape(n), slot * local, local, 0)]
where the time goes in v2:
time: 22.3 us; the launch traced here: 22.1 us
  Pallas kernels  21.5 us (96%)
  between operations  0.64 us (3%)
    pallas_call x1, Pallas kernels, on_device(): pl.pallas_call(functools.partial(spread_kernel, sizes), out_shape=(jax.Sh...  19.7 us
    pallas_call x1, Pallas kernels, on_device(): pl.pallas_call(functools.partial(sums_kernel, sizes), out_shape=(jax.Shap...  1.76 us

profile of v2, /device:TPU:0, one launch (start us, length us, event | category | flops | bytes accessed | tf_op | source)
XLA Modules:
  0.0 22.1 jit_solution(14867255467326873687)
XLA Ops:
  0.6 19.7 %shard_map.49 = (f32[1,256]{1,0:T(1,128)S(1)}, bf16[1024,256]{1,0:T(8,128)(2,1)S(1)}, bf16[256,1024]{1,0:T(8,128)(2,1)S(1)}) custom-call(bf16[8,1024]{1,0:T(8,128)(2,1)} %emb.1, bf16[1024,1024]{1,0:T(8,128)(2,1)} %cen.1), custom_call_target="tpu_custom_call" | custom-call | tf_op jit(solution)/shard_map/pallas_call | solution.py:233
  20.4 1.8 %shard_map.50 = (f32[1,8]{1,0:T(1,128)}, f32[1,1024]{1,0:T(1,128)}, bf16[1024,1024]{1,0:T(8,128)(2,1)}) custom-call(f32[1,256]{1,0:T(1,128)S(1)} %get-tuple-element.9.lse, bf16[1024,256]{1,0:T(8,128)(2,1)S(1)} %get-tuple-element.10.resp, bf16[256,1024]{1,0:T(8,128)(2,1)S(1)} %get-tuple-element.11.gathered), custom_call_target="tpu_custom_call" | custom-call | tf_op jit(solution)/shard_map/pallas_call | solution.py:256

commit v3 on v2

--- a/solution.py
+++ b/solution.py
@@ -33,7 +33,7 @@
 
 def spread_kernel(
     sizes, emb, cen, lse_out, resp, gathered,
-    cen_v, slots, shifted, stats,
+    cen_v, slots, shifted, tops, stats,
     own_sem, cen_sem, b_send, b_recv, c_send, c_recv, s_send, s_recv,
 ):
     Y, X, Z = sizes
@@ -90,8 +90,8 @@
     def to_plane(i, src):
         return [
             start(send(src, block_slot(i, 0), link_sems(i, p), p_peers[p]))
-            for p in range(1, len(plane))
-        ]
+            for p in range(len(plane) - 1, 0, -1)
+        ][::-1]
 
     def to_twin(i, p, src):
         return start(send(src, block_slot(i, p), (c_send.at[i, p], c_recv.at[i, p]), twin))
@@ -150,8 +150,8 @@
             part = jnp.exp(shifted[rows, lanes] - top)
             shifted[rows, lanes] = part
             total = total + jnp.sum(part.reshape(tile // 8, 8, wide), axis=0)
-        stats[me, 0:1, lanes] = top
-        stats[me, 1:2, lanes] = jnp.sum(total, axis=0, keepdims=True)
+        tops[:, lanes] = top
+        stats[me, :, lanes] = top + jnp.log(jnp.sum(total, axis=0, keepdims=True))
 
     offsets = [
         (i, j, l, m) for l in range(Z) for i in range(Y) for j in range(X) for m in range(2)
@@ -171,12 +171,11 @@
     @pl.loop(0, n // wide)
     def _(j):
         lanes = pl.ds(pl.multiple_of(j * wide, wide), wide)
-        tops = stats[:, 0:1, lanes]
-        top = jnp.max(tops, axis=0)
-        total = jnp.sum(stats[:, 1:2, lanes] * jnp.exp(tops - top[None]), axis=0)
-        lse = top + jnp.log(total)
+        part_lse = stats[:, :, lanes]
+        top = jnp.max(part_lse, axis=0)
+        lse = top + jnp.log(jnp.sum(jnp.exp(part_lse - top[None]), axis=0))
         lse_out[:, lanes] = lse
-        factor = jnp.exp(stats[me, 0:1, lanes] - lse)
+        factor = jnp.exp(tops[:, lanes] - lse)
         for t in range(k // tile):
             rows = pl.ds(t * tile, tile)
             resp[rows, lanes] = (shifted[rows, lanes] * factor).astype(jnp.bfloat16)
@@ -204,7 +203,7 @@
         ).astype(jnp.bfloat16)
         outs.append(pltpu.make_async_copy(sums_v.at[rows], sums_out.at[rows], out_sem.at[t]))
         outs[-1].start()
-        if t == 0:
+        if t == 1:
             rolled = pltpu.roll(jnp.broadcast_to(lse[...], (8, n)), n - slot * local, 1)
             lse_v[...] = rolled[0:1, :local]
             outs.append(pltpu.make_async_copy(lse_v, lse_out, lse_sem))
@@ -243,7 +242,8 @@
             pltpu.VMEM((k, depth), jnp.bfloat16),
             pltpu.VMEM((devices, local, depth), jnp.bfloat16),
             pltpu.VMEM((k, n), jnp.float32),
-            pltpu.VMEM((devices, 2, n), jnp.float32),
+            pltpu.VMEM((1, n), jnp.float32),
+            pltpu.VMEM((devices, 1, n), jnp.float32),
             dma, dma,
             dma((Z, Y * X)), dma((Z, Y * X)),
             dma((Z, Y * X)), dma((Z, Y * X)),

time: 22.3 us -> 21.8 us (0.978)
  Pallas kernels: 21.5 us -> 21 us
    pallas_call x1, Pallas kernels: 19.7 us -> 19.3 us  [on_device(): pl.pallas_call(functools.partial(spread_kernel, sizes), out_shape=(jax.Sh...]
where the time goes in v3:
time: 21.8 us; the launch traced here: 21.6 us
  Pallas kernels  21 us (96%)
  between operations  0.64 us (3%)
    pallas_call x1, Pallas kernels, on_device(): pl.pallas_call(functools.partial(spread_kernel, sizes), out_shape=(jax.Sh...  19.3 us
    pallas_call x1, Pallas kernels, on_device(): pl.pallas_call(functools.partial(sums_kernel, sizes), out_shape=(jax.Shap...  1.72 us

profile of v3, /device:TPU:0, one launch (start us, length us, event | category | flops | bytes accessed | tf_op | source)
XLA Modules:
  0.0 21.6 jit_solution(18127494612446020559)
XLA Ops:
  0.6 19.3 %shard_map.49 = (f32[1,256]{1,0:T(1,128)S(1)}, bf16[1024,256]{1,0:T(8,128)(2,1)S(1)}, bf16[256,1024]{1,0:T(8,128)(2,1)S(1)}) custom-call(bf16[8,1024]{1,0:T(8,128)(2,1)} %emb.1, bf16[1024,1024]{1,0:T(8,128)(2,1)} %cen.1), custom_call_target="tpu_custom_call" | custom-call | tf_op jit(solution)/shard_map/pallas_call | solution.py:232
  19.9 1.7 %shard_map.50 = (f32[1,8]{1,0:T(1,128)}, f32[1,1024]{1,0:T(1,128)}, bf16[1024,1024]{1,0:T(8,128)(2,1)}) custom-call(f32[1,256]{1,0:T(1,128)S(1)} %get-tuple-element.9.lse, bf16[1024,256]{1,0:T(8,128)(2,1)S(1)} %get-tuple-element.10.resp, bf16[256,1024]{1,0:T(8,128)(2,1)S(1)} %get-tuple-element.11.gathered), custom_call_target="tpu_custom_call" | custom-call | tf_op jit(solution)/shard_map/pallas_call | solution.py:256

commit v4 on v3

--- a/solution.py
+++ b/solution.py
@@ -65,7 +65,6 @@
     load_own = pltpu.make_async_copy(emb, slots.at[mine], own_sem)
     load_own.start()
     load = pltpu.make_async_copy(cen, cen_v, cen_sem)
-    load.start()
     pl.semaphore_wait(barrier, len(z_peers) + len(p_peers) - 1)
 
     def send(src, slot, sems, peer):
@@ -97,11 +96,14 @@
         return start(send(src, block_slot(i, p), (c_send.at[i, p], c_recv.at[i, p]), twin))
 
     arrivals = {}
+    load_own.wait()
+    emb = slots.at[mine]
     for i in range(Z - 1, 0, -1):
         arrivals[i, 0] = start(send(emb, mine, link_sems(i, 0), z_peers[i]))
     for p, copy in enumerate(to_plane(0, emb)):
         arrivals[0, p + 1] = copy
     over = [to_twin(0, 0, emb)]
+    load.start()
     for i in range(1, Z):
         arrivals[i, 0].wait_recv()
         src = slots.at[block_slot(i, 0)]
@@ -112,8 +114,6 @@
         for p in range(1, len(plane)):
             arrivals[i, p].wait_recv()
             over.append(to_twin(i, p, slots.at[block_slot(i, p)]))
-    load_own.wait()
-
     step = min(8, devices // 2)
 
     def lay_out(first):
@@ -154,7 +154,7 @@
         stats[me, :, lanes] = top + jnp.log(jnp.sum(total, axis=0, keepdims=True))
 
     offsets = [
-        (i, j, l, m) for l in range(Z) for i in range(Y) for j in range(X) for m in range(2)
+        (i, j, l, m) for m in range(2) for i in range(Y) for j in range(X) for l in range(Z)
     ]
     for i, j, l, m in reversed(offsets[1:]):
         peer = place(flipped(y, Y, i), (core + m) % 2, flipped(z, Z, l), flipped(x, X, j))

time: 21.8 us -> 21.4 us (0.982)
  Pallas kernels: 21 us -> 20.6 us
    pallas_call x1, Pallas kernels: 19.3 us -> 18.9 us  [on_device(): pl.pallas_call(functools.partial(spread_kernel, sizes), out_shape=(jax.Sh...]
where the time goes in v4:
time: 21.4 us; the launch traced here: 21.2 us
  Pallas kernels  20.6 us (96%)
  between operations  0.64 us (3%)
    pallas_call x1, Pallas kernels, on_device(): pl.pallas_call(functools.partial(spread_kernel, sizes), out_shape=(jax.Sh...  18.9 us
    pallas_call x1, Pallas kernels, on_device(): pl.pallas_call(functools.partial(sums_kernel, sizes), out_shape=(jax.Shap...  1.72 us

profile of v4, /device:TPU:0, one launch (start us, length us, event | category | flops | bytes accessed | tf_op | source)
XLA Modules:
  0.0 21.2 jit_solution(11653946516477193077)
XLA Ops:
  0.6 18.9 %shard_map.49 = (f32[1,256]{1,0:T(1,128)S(1)}, bf16[1024,256]{1,0:T(8,128)(2,1)S(1)}, bf16[256,1024]{1,0:T(8,128)(2,1)S(1)}) custom-call(bf16[8,1024]{1,0:T(8,128)(2,1)} %emb.1, bf16[1024,1024]{1,0:T(8,128)(2,1)} %cen.1), custom_call_target="tpu_custom_call" | custom-call | tf_op jit(solution)/shard_map/pallas_call | solution.py:232
  19.5 1.7 %shard_map.50 = (f32[1,8]{1,0:T(1,128)}, f32[1,1024]{1,0:T(1,128)}, bf16[1024,1024]{1,0:T(8,128)(2,1)}) custom-call(f32[1,256]{1,0:T(1,128)S(1)} %get-tuple-element.9.lse, bf16[1024,256]{1,0:T(8,128)(2,1)S(1)} %get-tuple-element.10.resp, bf16[256,1024]{1,0:T(8,128)(2,1)S(1)} %get-tuple-element.11.gathered), custom_call_target="tpu_custom_call" | custom-call | tf_op jit(solution)/shard_map/pallas_call | solution.py:256
